TPU v7x, 32 devices: a whole 2x2x4 slice. The times are simulated.
32 devices in a mesh: ctx: 8 (over y, x, core), tp: 4 (over z).
Axes of the slice: x: 2, y: 2, z: 4, core: 2. Of those that a mesh axis runs over, the one named last changes fastest.
Arguments:
- streams: bfloat16 [3, 2048, 2048], P(None, 'ctx', 'tp'), may hold values from -6 to 6
- short_filter: float32 [3, 7, 2048], P(None, None, 'tp'), may hold values from -2 to 2
- decay_rates: float32 [2048, 16], P('tp'), may hold values from 2.4414063e-05 to 0.05, as said below
- residues: float32 [2048, 16], P('tp'), may hold values from -0.06 to 0.06
- skip_gain: float32 [2048], P('tp'), may hold values from 0.5 to 1.5
- hyena_weight: bfloat16 [2048, 4096], P('tp'), may hold values from -0.1875 to 0.1875
- value_weight: bfloat16 [4096, 2048], P('tp'), may hold values from -0.125 to 0.125
- queries: bfloat16 [2048, 2048], P('ctx', 'tp'), may hold values from -16.5 to 16.5
- key_vectors: bfloat16 [2048, 2048], P('ctx', 'tp'), may hold values from -16.5 to 16.5
Outputs:
- hyena_out: bfloat16 [2048, 4096], P('ctx', 'tp')
- context: bfloat16 [2048, 2048], P('ctx', 'tp')
Inputs may be any that keep to these rules, and one draw needn't show every extreme that they name: `decay_rates`: decay rates lie between 1 / 40960 and 0.05.
All inputs are finite; a program needn't handle non-finite values.
Results may differ from a plain program's by a relative error of at most 0.0066.
Values may be sent and summed in bfloat16 or wider, within the bound.
A program may use at most 128 MiB of HBM per device.

v0:
```python
import functools
import math

import jax
import jax.numpy as jnp
from jax import lax
from jax.experimental import pallas as pl
from jax.experimental.pallas import tpu as pltpu
from jax.sharding import PartitionSpec as P

HD = 128
LANES = 128
SEGS = 8
HALO = 16


def from_behind(value, axis, steps):
    count = lax.axis_size(axis)
    initial, last = (max(0, -steps), min(count, count - steps))
    return lax.ppermute(value, axis, [(source, source + steps) for source in range(initial, last)])


def filter_kernel(prev_ref, streams_ref, taps_ref, rates_ref, gate_ref, u_ref, seg_ref, end_ref, ext):
    rows = streams_ref.shape[1]
    steps = rows // SEGS
    modes = rates_ref.shape[0]
    outs = []
    for s in range(3):
        ext[s, :HALO, :] = prev_ref[s].astype(jnp.float32)
        ext[s, HALO:, :] = streams_ref[s].astype(jnp.float32)
    for s in range(3):
        acc = taps_ref[s, 0:1, :] * ext[s, HALO:, :]
        for j in range(1, 7):
            acc = acc + taps_ref[s, j : j + 1, :] * ext[s, HALO - j : HALO - j + rows, :]
        outs.append(acc)
    gate_ref[...] = outs[0]
    u_ref[...] = outs[1] * outs[2]
    rates = rates_ref[...]
    decay = jnp.exp(-rates)
    factor = [jnp.broadcast_to(decay[n : n + 1], (SEGS, LANES)) for n in range(modes)]
    state = [jnp.zeros((SEGS, LANES), jnp.float32) for _ in range(modes)]
    for step in range(steps):
        here = u_ref[pl.ds(step, SEGS, stride=steps), :]
        for n in range(modes):
            state[n] = state[n] * factor[n] + here
    left = (steps * (SEGS - 1 - lax.broadcasted_iota(jnp.int32, (SEGS, LANES), 0))).astype(jnp.float32)
    for n in range(modes):
        seg_ref[n * SEGS : (n + 1) * SEGS, :] = state[n]
        reach = jnp.exp(-jnp.broadcast_to(rates[n : n + 1], (SEGS, LANES)) * left)
        end_ref[n : n + 1, :] = jnp.sum(reach * state[n], axis=0, keepdims=True)


def mix_kernel(gate_ref, u_ref, seg_ref, inc_ref, rates_ref, res_ref, skip_ref, out_ref, first, mixed):
    rows = u_ref.shape[0]
    steps = rows // SEGS
    modes = rates_ref.shape[0]
    rates = rates_ref[...]
    decay = jnp.exp(-rates)
    hop = jnp.exp(-rates * steps)
    carried = inc_ref[...]
    for seg in range(SEGS):
        first[pl.ds(seg, modes, stride=SEGS), :] = carried
        carried = carried * hop + seg_ref[pl.ds(seg, modes, stride=SEGS), :]
    residue = res_ref[...]
    skip = jnp.broadcast_to(skip_ref[...], (SEGS, LANES))
    factor = [jnp.broadcast_to(decay[n : n + 1], (SEGS, LANES)) for n in range(modes)]
    weight = [jnp.broadcast_to(residue[n : n + 1], (SEGS, LANES)) for n in range(modes)]
    state = [first[n * SEGS : (n + 1) * SEGS, :] for n in range(modes)]
    for step in range(steps):
        where = pl.ds(step, SEGS, stride=steps)
        here = u_ref[where, :]
        terms = [skip * here, None]
        for n in range(modes):
            state[n] = state[n] * factor[n] + here
            term = weight[n] * state[n]
            terms[n % 2] = term if terms[n % 2] is None else terms[n % 2] + term
        mixed[where, :] = gate_ref[where, :] * (terms[0] + terms[1])
    out_ref[...] = mixed[...].astype(jnp.bfloat16)


def hyena_gated(streams, short_filter, rates, residues, skip_gain):
    rows, chans = streams.shape[1:]
    modes = rates.shape[0]
    blocks = chans // LANES
    previous = from_behind(streams[:, rows - HALO :, :], "ctx", 1)
    f32 = jnp.float32
    tok = pl.BlockSpec((rows, LANES), lambda i: (0, i))
    pole = pl.BlockSpec((modes, LANES), lambda i: (0, i))
    seg = pl.BlockSpec((modes * SEGS, LANES), lambda i: (0, i))
    gate, u, seg_state, end_state = pl.pallas_call(
        filter_kernel,
        grid=(blocks,),
        in_specs=[
            pl.BlockSpec((3, HALO, LANES), lambda i: (0, 0, i)),
            pl.BlockSpec((3, rows, LANES), lambda i: (0, 0, i)),
            pl.BlockSpec((3, 7, LANES), lambda i: (0, 0, i)),
            pole,
        ],
        out_specs=[tok, tok, seg, pole],
        out_shape=[
            jax.ShapeDtypeStruct((rows, chans), f32),
            jax.ShapeDtypeStruct((rows, chans), f32),
            jax.ShapeDtypeStruct((modes * SEGS, chans), f32),
            jax.ShapeDtypeStruct((modes, chans), f32),
        ],
        scratch_shapes=[pltpu.VMEM((3, rows + HALO, LANES), f32)],
        cost_estimate=pl.CostEstimate(flops=20_000_000, bytes_accessed=2_500_000, transcendentals=0),
        compiler_params=pltpu.CompilerParams(vmem_limit_bytes=24 * 1024 * 1024),
        name="filter_scan",
    )(previous, streams, short_filter, rates)
    count, mine = lax.axis_size("ctx"), lax.axis_index("ctx")
    ends = lax.all_gather(end_state, "ctx")
    gap = mine - 1 - jnp.arange(count)
    reach = jnp.exp(-rates[None] * (rows * jnp.maximum(gap, 0)).astype(f32)[:, None, None])
    incoming = jnp.sum(jnp.where((gap >= 0)[:, None, None], reach * ends, 0.0), axis=0)
    return pl.pallas_call(
        mix_kernel,
        grid=(blocks,),
        in_specs=[tok, tok, seg, pole, pole, pole, pl.BlockSpec((1, LANES), lambda i: (0, i))],
        out_specs=tok,
        out_shape=jax.ShapeDtypeStruct((rows, chans), jnp.bfloat16),
        scratch_shapes=[pltpu.VMEM((modes * SEGS, LANES), f32), pltpu.VMEM((rows, LANES), f32)],
        cost_estimate=pl.CostEstimate(flops=20_000_000, bytes_accessed=2_500_000, transcendentals=0),
        compiler_params=pltpu.CompilerParams(vmem_limit_bytes=24 * 1024 * 1024),
        name="mix_scan",
    )(gate, u, seg_state, incoming, rates, residues, skip_gain[None])


def attend_kernel(
    ctx,
    tp,
    gated_ref,
    share_ref,
    weight_ref,
    q_ref,
    own_ref,
    hyena_ref,
    out_ref,
    gat,
    full,
    terms_ref,
    keys,
    parts,
    vals,
    acc,
    top,
    total,
    gat_sems,
    full_sems,
    key_sems,
    sum_sems,
    val_sems,
):
    rows, width = q_ref.shape
    heads = width // HD
    scale = 1.0 / math.sqrt(HD)
    me, lane = lax.axis_index("ctx"), lax.axis_index("tp")

    barrier = pltpu.get_barrier_semaphore()
    for away in range(1, tp):
        pl.semaphore_signal(
            barrier,
            inc=1,
            device_id={"tp": lax.rem(lane + away, tp)},
            device_id_type=pl.DeviceIdType.MESH,
        )
    for away in range(1, ctx):
        pl.semaphore_signal(
            barrier,
            inc=1,
            device_id={"ctx": lax.rem(me + away, ctx)},
            device_id_type=pl.DeviceIdType.MESH,
        )
    pl.semaphore_wait(barrier, tp - 1 + ctx - 1)

    def gat_copy(away):
        return pltpu.make_async_remote_copy(
            src_ref=gated_ref,
            dst_ref=gat.at[lane],
            send_sem=gat_sems.at[0, away],
            recv_sem=gat_sems.at[1, away],
            device_id={"tp": lax.rem(lane + away, tp)},
            device_id_type=pl.DeviceIdType.MESH,
        )

    chips = ctx // 2
    chip, core = lax.div(me, 2), lax.rem(me, 2)
    sibling = 2 * chip + 1 - core

    def full_copy(index):
        if index == 0:
            source, block, target = share_ref, me, sibling
        elif index < chips:
            source, block = share_ref, me
            target = 2 * lax.rem(chip + index, chips) + core
        else:
            away = index - chips + 1
            block = 2 * lax.rem(chip + chips - away, chips) + core
            source, target = full.at[:, block], sibling
        return pltpu.make_async_remote_copy(
            src_ref=source,
            dst_ref=full.at[:, block],
            send_sem=full_sems.at[0, index],
            recv_sem=full_sems.at[1, index],
            device_id={"ctx": target},
            device_id_type=pl.DeviceIdType.MESH,
        )

    def later(buffer, sems, source, slot, index, target):
        return pltpu.make_async_remote_copy(
            src_ref=buffer(source),
            dst_ref=buffer(slot),
            send_sem=sems(0, index),
            recv_sem=sems(1, slot),
            device_id={"ctx": target},
            device_id_type=pl.DeviceIdType.MESH,
        )

    def ahead(at, d):
        return later(*at, 0, 2 * d, 2 * d, lax.rem(me + 2 * d, ctx))

    def beside(at):
        return later(*at, 0, 1, 0, sibling)

    def onward(at, d):
        return later(*at, 2 * d, 2 * d + 1 - 2 * core, 2 * d - 1, sibling)

    def loop(first, last, act):
        def body(i, unused):
            act(i)
            return unused

        lax.fori_loop(first, last, body, 0)

    def give(at):
        loop(1, chips - chip, lambda d: ahead(at, d).start())
        loop(0, 1 - core, lambda d: beside(at).start())

    def relay(at):
        def step(d):
            ahead(at, d).wait_recv()
            onward(at, d).start()

        loop(1, chip + 1, step)

    def odd(at, i):
        return later(*at, 0, 2 * i + 1, 0, sibling)

    def take(at):
        loop(0, chip + core, lambda i: odd(at, i).wait_recv())

    def given(at):
        loop(1, chips - chip, lambda d: ahead(at, d).wait_send())
        loop(0, 1 - core, lambda d: beside(at).wait_send())
        loop(1, chip + 1, lambda d: onward(at, d).wait_send())

    key_at = (lambda slot: keys.at[slot], lambda way, i: key_sems.at[way, i])

    def val_at(head):
        return (lambda slot: vals.at[slot, head], lambda way, i: val_sems.at[way, i, head])

    for away in range(1, tp):
        gat_copy(away).start()
    for index in range(1, chips):
        full_copy(index).start()
    full_copy(0).start()

    gat[lane] = gated_ref[...]
    full[:, me] = share_ref[...]
    keys[0] = own_ref[...]
    for index in range(1, chips):
        full_copy(index).wait_recv()
        full_copy(index + chips - 1).start()
    give(key_at)
    for away in range(1, tp):
        gat_copy(away).wait_recv()
    full_copy(0).wait_recv()
    for index in range(chips, 2 * chips - 1):
        full_copy(index).wait_recv()
    chans, wide = gat.shape[2], full.shape[3]
    tile = min(wide, 256)
    for at in range(0, wide, tile):
        summed = None
        for p in range(tp):
            term = jnp.dot(
                gat[p],
                full[p, :, :, at : at + tile].reshape(chans, tile),
                preferred_element_type=jnp.float32,
            )
            summed = term if summed is None else summed + term
        hyena_ref[:, at : at + tile] = summed.astype(jnp.bfloat16)
    for at in range(0, tp * width, width):
        terms_ref[:, at : at + width] = jnp.dot(
            hyena_ref[...], weight_ref[:, at : at + width], preferred_element_type=jnp.float32
        ).astype(jnp.bfloat16)

    def columns(owner, head):
        return terms_ref.at[:, pl.ds(pl.multiple_of(owner * width + head * HD, HD), HD)]

    def sum_copy(away, head):
        owner = lax.rem(lane + away, tp)
        return pltpu.make_async_remote_copy(
            src_ref=columns(owner, head),
            dst_ref=parts.at[away - 1, head],
            send_sem=sum_sems.at[0, away - 1, head],
            recv_sem=sum_sems.at[1, away - 1, head],
            device_id={"tp": owner},
            device_id_type=pl.DeviceIdType.MESH,
        )

    for head in range(heads):
        for away in range(1, tp):
            sum_copy(away, head).start()

    def attend(head):
        here = slice(head * HD, (head + 1) * HD)

        def fold(behind, diagonal):
            scores = (
                lax.dot_general(
                    q_ref[:, here],
                    keys[behind, :, here],
                    (((1,), (1,)), ((), ())),
                    preferred_element_type=jnp.float32,
                )
                * scale
            )
            if diagonal:
                query = lax.broadcasted_iota(jnp.int32, (rows, rows), 0)
                key = lax.broadcasted_iota(jnp.int32, (rows, rows), 1)
                scores = jnp.where(key <= query, scores, -1e30)
                new = jnp.max(scores, axis=1, keepdims=True)
                weights = jnp.exp(scores - new)
                total[...] = jnp.broadcast_to(jnp.sum(weights, axis=1, keepdims=True), total.shape)
                kept = 0.0
            else:
                old = top[:, 0:1]
                new = jnp.maximum(old, jnp.max(scores, axis=1, keepdims=True))
                weights = jnp.exp(scores - new)
                rescale = jnp.exp(old - new)
                total[...] = jnp.broadcast_to(
                    total[:, 0:1] * rescale + jnp.sum(weights, axis=1, keepdims=True), total.shape
                )
                kept = acc[...] * rescale
            top[...] = jnp.broadcast_to(new, top.shape)
            acc[...] = kept + jnp.dot(
                weights.astype(jnp.bfloat16), vals[behind, head], preferred_element_type=jnp.float32
            )

        fold(0, True)

        def earlier(behind, unused):
            fold(behind, False)
            return unused

        lax.fori_loop(1, me + 1, earlier, 0)
        out_ref[:, here] = (acc[...] / total[...]).astype(jnp.bfloat16)

    for head in range(heads):
        value = columns(lane, head)[...].astype(jnp.float32)
        for away in range(1, tp):
            sum_copy(away, head).wait_recv()
            value = value + parts[away - 1, head].astype(jnp.float32)
        vals[0, head] = value.astype(jnp.bfloat16)

        give(val_at(head))
        if head == 0:
            relay(key_at)
            take(key_at)
        else:
            relay(val_at(head - 1))
            take(val_at(head - 1))
            attend(head - 1)
    relay(val_at(heads - 1))
    take(val_at(heads - 1))
    attend(heads - 1)

    for head in range(heads):
        for away in range(1, tp):
            sum_copy(away, head).wait_send()

        given(val_at(head))
    for away in range(1, tp):
        gat_copy(away).wait_send()
    for index in range(2 * chips - 1):
        full_copy(index).wait_send()

    given(key_at)


def sum_and_attend(gated, share, value_weight, queries, keys):
    ctx, tp = lax.axis_size("ctx"), lax.axis_size("tp")
    rows, width = queries.shape
    heads = width // HD
    return pl.pallas_call(
        functools.partial(attend_kernel, ctx, tp),
        in_specs=[pl.BlockSpec(memory_space=pltpu.VMEM)] * 5,
        out_specs=[pl.BlockSpec(memory_space=pltpu.VMEM)] * 2,
        out_shape=[
            jax.ShapeDtypeStruct((rows, share.shape[2]), jnp.bfloat16),
            jax.ShapeDtypeStruct((rows, width), jnp.bfloat16),
        ],
        scratch_shapes=[
            pltpu.VMEM((tp,) + gated.shape, jnp.bfloat16),
            pltpu.VMEM((tp, ctx) + share.shape[1:], jnp.bfloat16),
            pltpu.VMEM((rows, tp * width), jnp.bfloat16),
            pltpu.VMEM((ctx, rows, width), jnp.bfloat16),
            pltpu.VMEM((tp - 1, heads, rows, HD), jnp.bfloat16),
            pltpu.VMEM((ctx, heads, rows, HD), jnp.bfloat16),
            pltpu.VMEM((rows, HD), jnp.float32),
            pltpu.VMEM((rows, HD), jnp.float32),
            pltpu.VMEM((rows, HD), jnp.float32),
            pltpu.SemaphoreType.DMA((2, tp)),
            pltpu.SemaphoreType.DMA((2, ctx)),
            pltpu.SemaphoreType.DMA((2, ctx)),
            pltpu.SemaphoreType.DMA((2, tp - 1, heads)),
            pltpu.SemaphoreType.DMA((2, ctx, heads)),
        ],
        cost_estimate=pl.CostEstimate(
            flops=4 * rows * ctx * rows * width,
            bytes_accessed=4 * ctx * rows * width,
            transcendentals=0,
        ),
        compiler_params=pltpu.CompilerParams(
            vmem_limit_bytes=48 * 1024 * 1024, collective_id=0, has_side_effects=True
        ),
        name="sum_attend",
    )(gated, share, value_weight, queries, keys)


def shards(
    streams,
    short_filter,
    decay_rates,
    residues,
    skip_gain,
    hyena_weight,
    value_weight,
    queries,
    key_vectors,
):
    ctx, tp = lax.axis_size("ctx"), lax.axis_size("tp")
    rows = streams.shape[1]
    chans, width = hyena_weight.shape
    part = chans // ctx
    share = lax.dynamic_slice(hyena_weight, (lax.axis_index("ctx") * part, 0), (part, width))
    share = share.reshape(part, tp, width // tp).transpose(1, 0, 2)
    share = lax.all_to_all(share, "tp", split_axis=0, concat_axis=0, tiled=True)
    gated = hyena_gated(streams, short_filter, decay_rates.T, residues.T, skip_gain)
    hyena_out, context = sum_and_attend(gated, share, value_weight, queries, key_vectors)
    return (hyena_out, context)


def solution(mesh):
    return jax.shard_map(
        shards,
        mesh=mesh,
        in_specs=(
            P(None, "ctx", "tp"),
            P(None, None, "tp"),
            P("tp", None),
            P("tp", None),
            P("tp"),
            P("tp", None),
            P("tp", None),
            P("ctx", "tp"),
            P("ctx", "tp"),
        ),
        out_specs=(P("ctx", "tp"), P("ctx", "tp")),
        check_vma=False,
    )
```

profile of v0, /device:TPU:15, one launch (start us, length us, event | category | flops | bytes accessed | tf_op | source)
XLA Modules:
  0.0 106.0 jit_solution(17304491147270760642)
XLA Ops:
  0.6 0.0 copy-start.5
  0.6 0.0 copy-start.6
  0.7 0.0 copy-start.2
  0.7 0.0 copy-start.3
  0.7 1.1 %constant_dynamic-slice_fusion = bf16[64,4096]{1,0:T(8,128)(2,1)S(1)} fusion(bf16[512,4096]{1,0:T(8,128)(2,1)} %param.14, s32[]{:T(128)S(6)} %select_n.8), kind=kLoop, calls=%fused_computation.5 | loop fusion | bytes 1048580 | tf_op jit(solution)/shard_map/dynamic_slice | solution.py:446
  1.8 0.8 copy.14
  2.6 4.8 %all-to-all-start = ((bf16[4,64,1024]{2,1,0:T(8,128)(2,1)}), bf16[4,64,1024]{2,1,0:T(8,128)(2,1)S(1)}, u32[]{:S(2)}, u32[]{:S(2)}) async-start(bf16[4,64,1024]{2,1,0:T(8,128)(2,1)} %bitcast.11), calls=%async_computation | async-start | bytes 1048576 | tf_op jit(solution)/shard_map/all_to_all | solution.py:448
  7.4 0.8 slice.3
  8.2 1.3 %collective-permute-start = (bf16[3,16,512]{2,1,0:T(8,128)(2,1)S(1)}, bf16[3,16,512]{2,1,0:T(8,128)(2,1)S(1)}, u32[]{:S(2)}, u32[]{:S(2)}) collective-permute-start(bf16[3,16,512]{2,1,0:T(8,128)(2,1)S(1)} %slice.3), channel_id=1, source_target_pairs={{0,4},{4,8},{8,12},{12,16},{16,20},{20,24},{24,28},{1,5},{5,9},{9,... | collective-permute-start | bytes 147464 | tf_op jit(solution)/shard_map/ppermute | solution.py:20
  9.5 0.8 bitcast_negate_fusion
  10.3 1.8 %collective-permute-done.prev_ref = bf16[3,16,512]{2,1,0:T(8,128)(2,1)S(1)} collective-permute-done((bf16[3,16,512]{2,1,0:T(8,128)(2,1)S(1)}, bf16[3,16,512]{2,1,0:T(8,128)(2,1)S(1)}, u32[]{:S(2)}, u32[]{:S(2)}) %collective-permute-start) | collective-permute-done | bytes 49184 | tf_op jit(solution)/shard_map/ppermute | solution.py:20
  12.1 0.0 copy-start
  12.1 1.1 %copy-done = bf16[3,256,512]{2,1,0:T(8,128)(2,1)S(1)} copy-done((bf16[3,256,512]{2,1,0:T(8,128)(2,1)S(1)}, bf16[3,256,512]{2,1,0:T(8,128)(2,1)}, u32[]{:S(2)}) %copy-start) | copy-done | bytes 786456
  13.2 0.0 copy-start.1
  13.2 0.8 copy-done.1
  14.0 0.0 copy-start.4
  14.0 0.8 copy-done.4
  14.8 2.1 %filter_scan.1 = (f32[256,512]{1,0:T(8,128)S(1)}, f32[256,512]{1,0:T(8,128)S(1)}, f32[128,512]{1,0:T(8,128)S(1)}, f32[16,512]{1,0:T(8,128)S(1)}) custom-call(bf16[3,16,512]{2,1,0:T(8,128)(2,1)S(1)} %collective-permute-done.prev_ref, bf16[3,256,512]{2,1,0:T(8,128)(2,1)S(1)} %copy-done, f32[3,7,512]{2,1,0:T(8,128)S(1)} %copy-done.4, f32[16,512]{1,0:T(8,128)S(1)} %bitcast.12), custom_call_target="tpu_custom_call" | custom-call | flops 20000000 | bytes 2500000 | tf_op jit(solution)/shard_map/filter_scan/pallas_call | solution.py:90
  16.9 11.9 %all-gather = f32[128,512]{1,0:T(8,128)S(1)} all-gather(f32[16,512]{1,0:T(8,128)S(1)} %get-tuple-element.9), channel_id=2, replica_groups=mesh['ctx'=8,'tp'=4] {'ctx'}, dimensions={0}, use_global_device_ids=true | all-gather | bytes 294912 | tf_op jit(solution)/shard_map/all_gather | solution.py:112
  28.7 0.1 select_reduce_fusion.inc_ref
  28.8 0.0 copy-done.5
  28.8 0.0 copy-done.6
  28.9 2.1 %mix_scan.1.gated_ref = bf16[256,512]{1,0:T(8,128)(2,1)S(1)} custom-call(f32[256,512]{1,0:T(8,128)S(1)} %get-tuple-element.6.gate_ref, f32[256,512]{1,0:T(8,128)S(1)} %get-tuple-element.7.u_ref, f32[128,512]{1,0:T(8,128)S(1)} %get-tuple-element.8.seg_ref, f32[16,512]{1,0:T(8,128)S(1)} %select_reduce_fusion.inc_ref, f32[16,512]{1,0:T(8,128)S(1)} %bitcast.13, ...), custom_call_target="tpu_custom_call" | custom-call | flops 20000000 | bytes 2500000 | tf_op jit(solution)/shard_map/mix_scan/pallas_call | solution.py:116
  30.9 0.0 all-to-all-done.share_ref
  31.0 0.0 copy-done.2
  31.0 0.0 copy-done.3
  31.0 73.5 %sum_attend.1 = (bf16[256,1024]{1,0:T(8,128)(2,1)S(1)}, bf16[256,512]{1,0:T(8,128)(2,1)S(1)}) custom-call(bf16[256,512]{1,0:T(8,128)(2,1)S(1)} %mix_scan.1.gated_ref, bf16[4,64,1024]{2,1,0:T(8,128)(2,1)S(1)} %all-to-all-done.share_ref, bf16[1024,2048]{1,0:T(8,128)(2,1)} %weight_ref.1, bf16[256,512]{1,0:T(8,128)(2,1)S(1)} %copy-done.2, ...), custom_call_target="tpu_custom_call" | custom-call | flops 1073741824 | bytes 4194304 | tf_op jit(solution)/shard_map/sum_attend/pallas_call | solution.py:395
  104.5 0.8 copy.17
  105.3 0.7 copy.18
  (2 shorter events, 0.0 us)
Async XLA Ops:
  0.6 28.2 %copy-start.5 = (f32[512,16]{0,1:T(8,128)S(1)}, f32[512,16]{0,1:T(8,128)}, u32[]{:S(2)}) copy-start(f32[512,16]{0,1:T(8,128)} %param.12) | copy-start | bytes 98308
  0.6 28.2 %copy-start.6 = (f32[512]{0:T(512)S(1)}, f32[512]{0:T(512)}, u32[]{:S(2)}) copy-start(f32[512]{0:T(512)} %param.13) | copy-start | bytes 6148
  0.7 30.3 %copy-start.2 = (bf16[256,512]{1,0:T(8,128)(2,1)S(1)}, bf16[256,512]{1,0:T(8,128)(2,1)}, u32[]{:S(2)}) copy-start(bf16[256,512]{1,0:T(8,128)(2,1)} %q_ref.1) | copy-start | bytes 786436
  0.7 30.3 %copy-start.3 = (bf16[256,512]{1,0:T(8,128)(2,1)S(1)}, bf16[256,512]{1,0:T(8,128)(2,1)}, u32[]{:S(2)}) copy-start(bf16[256,512]{1,0:T(8,128)(2,1)} %own_ref.1) | copy-start | bytes 786436
  2.6 28.3 %all-to-all-start = ((bf16[4,64,1024]{2,1,0:T(8,128)(2,1)}), bf16[4,64,1024]{2,1,0:T(8,128)(2,1)S(1)}, u32[]{:S(2)}, u32[]{:S(2)}) async-start(bf16[4,64,1024]{2,1,0:T(8,128)(2,1)} %bitcast.11), calls=%async_computation | async-start | bytes 1048576 | tf_op jit(solution)/shard_map/all_to_all | solution.py:448
  8.2 3.9 %collective-permute-start = (bf16[3,16,512]{2,1,0:T(8,128)(2,1)S(1)}, bf16[3,16,512]{2,1,0:T(8,128)(2,1)S(1)}, u32[]{:S(2)}, u32[]{:S(2)}) collective-permute-start(bf16[3,16,512]{2,1,0:T(8,128)(2,1)S(1)} %slice.3), channel_id=1, source_target_pairs={{0,4},{4,8},{8,12},{12,16},{16,20},{20,24},{24,28},{1,5},{5,9},{9,... | collective-permute-start | bytes 147464 | tf_op jit(solution)/shard_map/ppermute | solution.py:20
  12.1 1.1 %copy-start = (bf16[3,256,512]{2,1,0:T(8,128)(2,1)S(1)}, bf16[3,256,512]{2,1,0:T(8,128)(2,1)}, u32[]{:S(2)}) copy-start(bf16[3,256,512]{2,1,0:T(8,128)(2,1)} %streams_ref.1) | copy-start | bytes 2359300
  13.2 0.8 copy-start.1
  14.0 0.8 copy-start.4
where the time goes:
time: 107 us; the launch traced here: 106 us
  Pallas kernels  77.7 us (73%)
  blocking collectives  11.9 us (11%)
  local copies, waits for them, and re-layouts  6.97 us (7%)
  starting transfers between devices  6.04 us (6%)
  waiting for transfers between devices  1.77 us (2%)
    pallas_call x1, Pallas kernels, sum_and_attend(): pl.pallas_call(functools.partial(attend_kernel, ctx, tp), in_specs=[pl.Bl...  73.5 us
    all_gather x1, blocking collectives, hyena_gated(): ends = lax.all_gather(end_state, 'ctx')  11.9 us
    all_to_all x1, starting transfers between devices, shards(): share = lax.all_to_all(share, 'tp', split_axis=0, concat_axis=0, tiled=True)  4.76 us
    unnamed x16, local copies, waits for them, and re-layouts  4.2 us
  transfers between devices with their start and end apart: 2, of which 1 were waited for; matrix products, arithmetic and copies ran while one was open for 2% of the time, Pallas kernels for 4%

commit v1 on v0

v1 whole, which is shorter than its diff:
```python
import functools
import math

import jax
import jax.numpy as jnp
from jax import lax
from jax.experimental import pallas as pl
from jax.experimental.pallas import tpu as pltpu
from jax.sharding import PartitionSpec as P

HD = 128
LANES = 128
SEGS = 8
HALO = 16
HALVES = 2
MESH = pl.DeviceIdType.MESH


def remote(source, target, send, recv, device):
    return pltpu.make_async_remote_copy(
        src_ref=source,
        dst_ref=target,
        send_sem=send,
        recv_sem=recv,
        device_id=device,
        device_id_type=MESH,
    )


class Grid:
    def __init__(self, ctx, me):
        self.side = math.isqrt(ctx // 2)
        assert 2 * self.side * self.side == ctx
        self.me = me
        self.chip, self.core = lax.div(me, 2), lax.rem(me, 2)
        self.a, self.b = lax.div(self.chip, self.side), lax.rem(self.chip, self.side)

    def at(self, first, second):
        da = first * self.core + second * (1 - self.core)
        db = second * self.core + first * (1 - self.core)
        chip = lax.rem(self.a + da, self.side) * self.side + lax.rem(self.b + db, self.side)
        return 2 * chip + self.core

    def sibling(self):
        return 2 * self.chip + 1 - self.core


class Gather:
    def __init__(self, grid, block, send, recv):
        self.grid, self.block, self.send, self.recv = grid, block, send, recv
        self.sent = []

    def push(self, owner, target):
        copy = remote(
            self.block(owner), self.block(owner), self.send(len(self.sent)), self.recv(owner), {"ctx": target}
        )
        copy.start()
        self.sent.append(copy)

    def wait(self, owner):
        remote(
            self.block(owner), self.block(owner), self.send(0), self.recv(owner), {"ctx": self.grid.sibling()}
        ).wait_recv()

    def own(self):
        grid = self.grid
        for k in range(1, grid.side):
            self.push(grid.me, grid.at(k, 0))
            self.push(grid.me, grid.at(0, k))
        self.push(grid.me, grid.sibling())

    def relay_first(self):
        grid = self.grid
        for k in range(1, grid.side):
            owner = grid.at(k, 0)
            self.wait(owner)
            for j in range(1, grid.side):
                self.push(owner, grid.at(0, j))
            self.push(owner, grid.sibling())

    def relay_second(self):
        grid = self.grid
        for j in range(1, grid.side):
            owner = grid.at(0, j)
            self.wait(owner)
            self.push(owner, grid.sibling())
        for j in range(1, grid.side):
            for k in range(1, grid.side):
                owner = grid.at(k, j)
                self.wait(owner)
                self.push(owner, grid.sibling())

    def take(self):
        grid = self.grid
        self.wait(grid.sibling())
        for j in range(grid.side):
            for k in range(grid.side):
                if j or k:
                    self.wait(grid.at(k, j) + 1 - 2 * grid.core)

    def finish(self):
        for copy in self.sent:
            copy.wait_send()


def sends_of(ctx):
    return ctx - 1


def body(
    ctx,
    tp,
    streams_hbm,
    taps_hbm,
    rates_hbm,
    res_hbm,
    skip_hbm,
    w_hbm,
    v_hbm,
    q_hbm,
    k_hbm,
    hyena_ref,
    out_ref,
    streams,
    prev,
    taps,
    rates_ref,
    residues,
    skips,
    ext,
    gate,
    u,
    seg,
    first,
    ends,
    gat,
    wfull,
    vv,
    q_ref,
    keys,
    vals,
    hacc,
    own_terms,
    snd,
    from_left,
    from_right,
    scores,
    probs,
    tops,
    totals,
    loc_sems,
    halo_sems,
    end_sems,
    wz_sems,
    wx_send,
    wx_recv,
    key_send,
    key_recv,
    val_send,
    val_recv,
    gat_send,
    gat_recv,
    sum_send,
    sum_recv,
):
    rows, width = q_ref.shape
    chans = streams.shape[2]
    blocks = chans // LANES
    half = rows // HALVES
    heads = width // HD
    modes = rates_ref.shape[0]
    steps = rows // SEGS
    wide = wfull.shape[3]
    f32 = jnp.float32
    me, z = lax.axis_index("ctx"), lax.axis_index("tp")
    grid = Grid(ctx, me)

    loads = [
        pltpu.make_async_copy(streams_hbm, streams, loc_sems.at[0]),
        pltpu.make_async_copy(taps_hbm, taps, loc_sems.at[1]),
        pltpu.make_async_copy(rates_hbm, rates_ref, loc_sems.at[2]),
        pltpu.make_async_copy(res_hbm, residues, loc_sems.at[3]),
        pltpu.make_async_copy(skip_hbm, skips, loc_sems.at[4]),
        pltpu.make_async_copy(k_hbm, keys.at[me], loc_sems.at[5]),
        pltpu.make_async_copy(q_hbm, q_ref, loc_sems.at[6]),
        pltpu.make_async_copy(
            w_hbm.at[:, :, pl.ds(pl.multiple_of(z * wide, wide), wide)], wfull.at[z], loc_sems.at[7]
        ),
    ] + [
        pltpu.make_async_copy(v_hbm.at[:, pl.ds(d * width, width)], vv.at[d], loc_sems.at[8 + d])
        for d in range(tp)
    ]
    for load in loads[:7]:
        load.start()

    barrier = pltpu.get_barrier_semaphore()
    for away in range(1, ctx):
        pl.semaphore_signal(barrier, inc=1, device_id={"ctx": lax.rem(me + away, ctx)}, device_id_type=MESH)
    for away in range(1, tp):
        pl.semaphore_signal(barrier, inc=1, device_id={"tp": lax.rem(z + away, tp)}, device_id_type=MESH)
    pl.semaphore_wait(barrier, tp - 1 + ctx - 1)

    halo = remote(
        streams_hbm.at[:, pl.ds(rows - HALO, HALO), :],
        prev,
        halo_sems.at[0],
        halo_sems.at[1],
        {"ctx": jnp.minimum(me + 1, ctx - 1)},
    )

    @pl.when(me < ctx - 1)
    def _():
        halo.start()

    shorter = jnp.minimum(z, tp - 1 - z)
    longer_way = jnp.where(z < tp - 1 - z, 1, -1)

    def near(j):
        paired = z + (j // 2 + 1) * (1 if j % 2 else -1)
        return jnp.where(j < 2 * shorter, paired, z + (j - shorter + 1) * longer_way)

    def w_copy(j):
        other = near(j)
        return remote(
            w_hbm.at[me, :, pl.ds(pl.multiple_of(other * wide, wide), wide)],
            wfull.at[z, me],
            wz_sems.at[0, j],
            wz_sems.at[1, z],
            {"tp": other},
        )

    def w_wait(j):
        source = near(j)
        remote(
            w_hbm.at[me, :, pl.ds(0, wide)], wfull.at[source, me], wz_sems.at[0, j], wz_sems.at[1, source], {"tp": source}
        ).wait_recv()

    def w_gather(j):
        source = near(j)
        return Gather(
            grid,
            lambda o: wfull.at[source, o],
            lambda i: wx_send.at[j, i],
            lambda o: wx_recv.at[j, o],
        )

    others = range(tp - 1)
    hops = range(1, tp)
    w_parts = [w_gather(j) for j in others]
    for j in others:
        w_copy(j).start()
    for load in loads[7:]:
        load.start()

    key_part = Gather(grid, lambda o: keys.at[o], lambda i: key_send.at[i], lambda o: key_recv.at[o])

    def val_gather(h):
        return Gather(
            grid, lambda o: vals.at[o, h], lambda i: val_send.at[h, i], lambda o: val_recv.at[h, o]
        )

    val_parts = [val_gather(h) for h in range(HALVES)]

    for load in loads[:5]:
        load.wait()

    @pl.when(me == 0)
    def _():
        prev[...] = jnp.zeros_like(prev)

    @pl.when(me > 0)
    def _():
        halo.wait_recv()

    def lanes_of(i):
        return pl.ds(pl.multiple_of(i * LANES, LANES), LANES)

    def pole_rows(value, n):
        return jnp.broadcast_to(value[n : n + 1], (SEGS, LANES))

    def filter_block(i, unused):
        at = lanes_of(i)
        outs = []
        for s in range(3):
            ext[s, :HALO, :] = prev[s, :, at].astype(f32)
            ext[s, HALO:, :] = streams[s, :, at].astype(f32)
        for s in range(3):
            tap = taps[s, :, at]
            acc = tap[0:1] * ext[s, HALO:, :]
            for j in range(1, 7):
                acc = acc + tap[j : j + 1] * ext[s, HALO - j : HALO - j + rows, :]
            outs.append(acc)
        gate[i] = outs[0]
        u[i] = outs[1] * outs[2]
        rates = rates_ref[:, at]
        decay = jnp.exp(-rates)
        factor = [pole_rows(decay, n) for n in range(modes)]
        state = [jnp.zeros((SEGS, LANES), f32) for _ in range(modes)]
        for step in range(steps):
            here = u[i, pl.ds(step, SEGS, stride=steps), :]
            for n in range(modes):
                state[n] = state[n] * factor[n] + here
        left = (steps * (SEGS - 1 - lax.broadcasted_iota(jnp.int32, (SEGS, LANES), 0))).astype(f32)
        for n in range(modes):
            seg[i, n * SEGS : (n + 1) * SEGS, :] = state[n]
            reach = jnp.exp(-pole_rows(rates, n) * left)
            ends[me, i, n : n + 1, :] = jnp.sum(reach * state[n], axis=0, keepdims=True)
        return unused

    lax.fori_loop(0, blocks, filter_block, 0)

    def end_copy(away):
        return remote(
            ends.at[me],
            ends.at[me],
            end_sems.at[0, away],
            end_sems.at[1, me],
            {"ctx": jnp.minimum(me + away, ctx - 1)},
        )

    def end_wait(o):
        remote(ends.at[o], ends.at[o], end_sems.at[0, 0], end_sems.at[1, o], {"ctx": grid.sibling()}).wait_recv()

    def each(count, act):
        def step(i, unused):
            act(i)
            return unused

        lax.fori_loop(0, count, step, 0)

    each(ctx - 1 - me, lambda i: end_copy(i + 1).start())
    w_wait(0)
    w_parts[0].own()
    each(me, end_wait)

    def mix_block(i, unused):
        at = lanes_of(i)
        rates = rates_ref[:, at]
        decay = jnp.exp(-rates)
        slab = jnp.exp(-rates * rows)
        hop = jnp.exp(-rates * steps)
        carried = lax.fori_loop(0, me, lambda o, c: c * slab + ends[o, i], jnp.zeros((modes, LANES), f32))
        for s in range(SEGS):
            first[pl.ds(s, modes, stride=SEGS), :] = carried
            carried = carried * hop + seg[i, pl.ds(s, modes, stride=SEGS), :]
        residue = residues[:, at]
        skip = jnp.broadcast_to(skips[:, at], (SEGS, LANES))
        factor = [pole_rows(decay, n) for n in range(modes)]
        weight = [pole_rows(residue, n) for n in range(modes)]
        state = [first[n * SEGS : (n + 1) * SEGS, :] for n in range(modes)]
        for step in range(steps):
            where = pl.ds(step, SEGS, stride=steps)
            here = u[i, where, :]
            terms = [skip * here, None]
            for n in range(modes):
                state[n] = state[n] * factor[n] + here
                term = weight[n] * state[n]
                terms[n % 2] = term if terms[n % 2] is None else terms[n % 2] + term
            gate[i, where, :] = gate[i, where, :] * (terms[0] + terms[1])
        for h in range(HALVES):
            gat[z, h, :, at] = gate[i, h * half : (h + 1) * half, :].astype(jnp.bfloat16)
        return unused

    lax.fori_loop(0, blocks, mix_block, 0)

    def gat_copy(source, h, way):
        return remote(
            gat.at[source, h],
            gat.at[source, h],
            gat_send.at[h, way, source],
            gat_recv.at[h, source],
            {"tp": jnp.clip(z + 1 - 2 * way, 0, tp - 1)},
        )

    def gat_give(source, h, way):
        @pl.when((z < tp - 1) if way == 0 else (z > 0))
        def _():
            gat_copy(source, h, way).start()

    def gat_own(h):
        for way in range(2):
            gat_give(z, h, way)

    def project(source, h, start):
        term = jnp.dot(
            gat[source, h], wfull[source].reshape(chans, wide), preferred_element_type=f32
        )
        if start:
            hacc[...] = term
        else:
            hacc[...] += term

    def gat_step(h, j):
        source = near(j)
        gat_copy(source, h, 0).wait_recv()

        @pl.when((source < z) & (z < tp - 1))
        def _():
            gat_copy(source, h, 0).start()

        @pl.when((source > z) & (z > 0))
        def _():
            gat_copy(source, h, 1).start()

    def all_terms(h):
        hyena = hacc[...].astype(jnp.bfloat16)
        hyena_ref[h * half : (h + 1) * half, :] = hyena
        for d in range(tp):
            own_terms[d] = jnp.dot(
                hyena_ref[h * half : (h + 1) * half, :], vv[d], preferred_element_type=f32
            )

    def sum_copy(d, h, way):
        box = from_left if way == 0 else from_right
        return remote(
            snd.at[h, d],
            box.at[h, d],
            sum_send.at[h, d],
            sum_recv.at[h, way, d],
            {"tp": jnp.clip(z + 1 - 2 * way, 0, tp - 1)},
        )

    def sum_step(h, k):
        for way in range(2):
            d = z + k if way == 0 else z - k

            @pl.when((d < tp) if way == 0 else (d >= 0))
            def _():
                box = from_left if way == 0 else from_right

                @pl.when((z > 0) if way == 0 else (z < tp - 1))
                def _():
                    sum_copy(d, h, way).wait_recv()
                    own_terms[d] += box[h, d].astype(f32)

                snd[h, d] = own_terms[d].astype(jnp.bfloat16)
                sum_copy(d, h, way).start()

    def sum_last(h):
        for way in range(2):
            box = from_left if way == 0 else from_right

            @pl.when((z > 0) if way == 0 else (z < tp - 1))
            def _():
                sum_copy(z, h, way).wait_recv()
                own_terms[z] += box[h, z].astype(f32)

        vals[me, h] = own_terms[z].astype(jnp.bfloat16)
        val_parts[h].own()

    scale = math.log2(math.e) / math.sqrt(HD)

    def weigh(head):
        here = slice(head * HD, (head + 1) * HD)

        def score(b):
            return (
                lax.dot_general(
                    q_ref[:, here], keys[b, :, here], (((1,), (1,)), ((), ())), preferred_element_type=f32
                )
                * scale
            )

        def fold(value, act):
            part = value[:, :HD]
            for at in range(HD, rows, HD):
                part = act(part, value[:, at : at + HD])
            return part

        query = lax.broadcasted_iota(jnp.int32, (rows, rows), 0)
        key = lax.broadcasted_iota(jnp.int32, (rows, rows), 1)
        mine = jnp.where(key <= query, score(me), -1e30)
        scores[me] = mine
        tops[...] = fold(mine, jnp.maximum)

        def earlier(b):
            value = score(b)
            scores[b] = value
            tops[...] = jnp.maximum(tops[...], fold(value, jnp.maximum))

        each(me, earlier)
        top = jnp.max(tops[...], axis=1, keepdims=True)
        tops[...] = jnp.broadcast_to(top, tops.shape)
        totals[head] = jnp.zeros_like(tops)

        def weight(b):
            value = jnp.exp2(scores[b] - tops[:, 0:1])
            totals[head] += fold(value, jnp.add)
            probs[head, b] = value.astype(jnp.bfloat16)

        each(me + 1, weight)
        totals[head] = jnp.broadcast_to(jnp.sum(totals[head], axis=1, keepdims=True), tops.shape)

    def blend(head):
        here = slice(head * HD, (head + 1) * HD)

        def step(b, acc):
            return acc + jnp.dot(
                probs[head, b], vals[b, :, :, here].reshape(rows, HD), preferred_element_type=f32
            )

        acc = lax.fori_loop(0, me + 1, step, jnp.zeros((rows, HD), f32))
        out_ref[:, here] = (acc / totals[head]).astype(jnp.bfloat16)

    loads[5].wait()
    gat_own(0)
    gat_own(1)
    w_wait(1)
    w_parts[1].own()
    w_parts[0].relay_first()
    for j in others[2:]:
        w_wait(j)
        w_parts[j].own()
    for j in others[1:]:
        w_parts[j].relay_first()
    gat_step(0, 0)
    key_part.own()
    for j in others:
        w_parts[j].relay_second()
    for load in loads[6:]:
        load.wait()
    project(z, 0, True)
    for j in others[1:]:
        gat_step(0, j)
    for j in others:
        w_parts[j].take()
        project(near(j), 0, False)
    all_terms(0)
    gat_step(1, 0)
    sum_step(0, tp - 1)
    key_part.relay_first()
    for j in others[1:]:
        gat_step(1, j)
        sum_step(0, tp - 1 - j)
    key_part.relay_second()
    project(z, 1, True)
    for j in others:
        project(near(j), 1, False)
    sum_last(0)
    all_terms(1)
    for k in reversed(hops):
        sum_step(1, k)
        if k == tp - 1:
            val_parts[0].relay_first()
            key_part.take()
    val_parts[0].relay_second()
    val_parts[0].take()
    for head in range(heads):
        weigh(head)
    sum_last(1)
    val_parts[1].relay_first()
    val_parts[1].relay_second()
    val_parts[1].take()
    for head in range(heads):
        blend(head)

    @pl.when(me < ctx - 1)
    def _():
        halo.wait_send()

    each(ctx - 1 - me, lambda i: end_copy(i + 1).wait_send())
    for j in others:
        w_copy(j).wait_send()
        w_parts[j].finish()
    key_part.finish()
    for h in range(HALVES):
        val_parts[h].finish()
        for way in range(2):

            @pl.when((z < tp - 1) if way == 0 else (z > 0))
            def _():
                gat_copy(z, h, way).wait_send()

        for j in others:
            source = near(j)

            @pl.when((source < z) & (z < tp - 1))
            def _():
                gat_copy(source, h, 0).wait_send()

            @pl.when((source > z) & (z > 0))
            def _():
                gat_copy(source, h, 1).wait_send()

        for k in hops:
            for way in range(2):
                d = z + k if way == 0 else z - k

                @pl.when((d < tp) if way == 0 else (d >= 0))
                def _():
                    sum_copy(d, h, way).wait_send()


def shards(streams, short_filter, decay_rates, residues, skip_gain, hyena_weight, value_weight, queries, key_vectors):
    ctx, tp = lax.axis_size("ctx"), lax.axis_size("tp")
    rows, chans = streams.shape[1:]
    width = queries.shape[1]
    wide = hyena_weight.shape[1] // tp
    deep = value_weight.shape[0]
    part = chans // ctx
    modes = decay_rates.shape[1]
    taps = short_filter.shape[1]
    blocks = chans // LANES
    heads = width // HD
    half = rows // HALVES
    f32, bf16 = jnp.float32, jnp.bfloat16
    dma = pltpu.SemaphoreType.DMA
    vmem = pltpu.VMEM
    return pl.pallas_call(
        functools.partial(body, ctx, tp),
        in_specs=[pl.BlockSpec(memory_space=pltpu.HBM)] * 9,
        out_specs=[pl.BlockSpec(memory_space=pltpu.VMEM)] * 2,
        out_shape=[
            jax.ShapeDtypeStruct((rows, wide), bf16),
            jax.ShapeDtypeStruct((rows, width), bf16),
        ],
        scratch_shapes=[
            vmem((3, rows, chans), bf16),
            vmem((3, HALO, chans), bf16),
            vmem((3, taps, chans), f32),
            vmem((modes, chans), f32),
            vmem((modes, chans), f32),
            vmem((1, chans), f32),
            vmem((3, rows + HALO, LANES), f32),
            vmem((blocks, rows, LANES), f32),
            vmem((blocks, rows, LANES), f32),
            vmem((blocks, modes * SEGS, LANES), f32),
            vmem((modes * SEGS, LANES), f32),
            vmem((ctx, blocks, modes, LANES), f32),
            vmem((tp, HALVES, half, chans), bf16),
            vmem((tp, ctx, part, wide), bf16),
            vmem((tp, deep, width), bf16),
            vmem((rows, width), bf16),
            vmem((ctx, rows, width), bf16),
            vmem((ctx, HALVES, half, width), bf16),
            vmem((half, wide), f32),
            vmem((tp, half, width), f32),
            vmem((HALVES, tp, half, width), bf16),
            vmem((HALVES, tp, half, width), bf16),
            vmem((HALVES, tp, half, width), bf16),
            vmem((ctx, rows, rows), f32),
            vmem((heads, ctx, rows, rows), bf16),
            vmem((rows, HD), f32),
            vmem((heads, rows, HD), f32),
            dma((8 + tp,)),
            dma((2,)),
            dma((2, ctx)),
            dma((2, tp)),
            dma((tp, ctx)),
            dma((tp, ctx)),
            dma((ctx,)),
            dma((ctx,)),
            dma((HALVES, ctx)),
            dma((HALVES, ctx)),
            dma((HALVES, 2, tp)),
            dma((HALVES, tp)),
            dma((HALVES, tp)),
            dma((HALVES, 2, tp)),
        ],
        cost_estimate=pl.CostEstimate(
            flops=4 * rows * ctx * rows * width,
            bytes_accessed=4 * ctx * rows * width,
            transcendentals=0,
        ),
        compiler_params=pltpu.CompilerParams(
            vmem_limit_bytes=56 * 1024 * 1024, collective_id=0, has_side_effects=True
        ),
        name="hyena_attention",
    )(
        streams,
        short_filter,
        decay_rates.T,
        residues.T,
        skip_gain[None],
        hyena_weight.reshape(ctx, part, tp * wide),
        value_weight,
        queries,
        key_vectors,
    )


def solution(mesh):
    return jax.shard_map(
        shards,
        mesh=mesh,
        in_specs=(
            P(None, "ctx", "tp"),
            P(None, None, "tp"),
            P("tp", None),
            P("tp", None),
            P("tp"),
            P("tp", None),
            P("tp", None),
            P("ctx", "tp"),
            P("ctx", "tp"),
        ),
        out_specs=(P("ctx", "tp"), P("ctx", "tp")),
        check_vma=False,
    )
```

time: 107 us -> 89 us (0.83)
  the two profiles are of different devices: /device:TPU:15 before, /device:TPU:0 now
where the time goes in v1:
time: 89 us; the launch traced here: 88.8 us
  Pallas kernels  84.6 us (95%)
  local copies, waits for them, and re-layouts  3.54 us (4%)
    pallas_call x1, Pallas kernels, shards(): pl.pallas_call(functools.partial(body, ctx, tp), in_specs=[pl.BlockSpec(m...  84.6 us
    unnamed x2, local copies, waits for them, and re-layouts  3.54 us

profile of v1, /device:TPU:0, one launch (start us, length us, event | category | flops | bytes accessed | tf_op | source)
XLA Modules:
  0.0 88.8 jit_solution(4315834275411194961)
XLA Ops:
  0.6 84.6 %hyena_attention.1 = (bf16[256,1024]{1,0:T(8,128)(2,1)}, bf16[256,512]{1,0:T(8,128)(2,1)}) custom-call(bf16[3,256,512]{2,1,0:T(8,128)(2,1)} %streams_hbm.1, f32[3,7,512]{2,1,0:T(8,128)} %taps_hbm.1, f32[16,512]{1,0:T(8,128)} %bitcast.5, f32[16,512]{1,0:T(8,128)} %bitcast.6, f32[1,512]{1,0:T(1,128)} %bitcast.7, bf16[8,64,4096]{2,1,0:T(8,128)(2,1)} %bitcast.4, ...), custom_call_target="tpu_custom_call" | custom-call | flops 1073741824 | bytes 4194304 | tf_op jit(solution)/shard_map/hyena_attention/pallas_call | solution.py:609
  85.2 1.9 %copy.13 = bf16[256,1024]{1,0:T(8,128)(2,1)} copy(bf16[256,1024]{1,0:T(8,128)(2,1)} %get-tuple-element.4) | data formatting | bytes 1048576
  87.1 1.7 %copy.14 = bf16[256,512]{1,0:T(8,128)(2,1)} copy(bf16[256,512]{1,0:T(8,128)(2,1)} %get-tuple-element.5) | data formatting | bytes 524288

commit v2 on v1

--- a/solution.py
+++ b/solution.py
@@ -13,6 +13,9 @@
 SEGS = 8
 HALO = 16
 HALVES = 2
+GAT_CUTS = 1
+W_CUTS = 2
+SUM_CUTS = 1
 MESH = pl.DeviceIdType.MESH
 
 
@@ -64,6 +67,14 @@
 
     def own(self):
         grid = self.grid
+        for j in reversed(range(grid.side)):
+            for k in reversed(range(grid.side)):
+                if j or k:
+                    self.push(grid.me, grid.at(k, j))
+        self.push(grid.me, grid.sibling())
+
+    def own_lines(self):
+        grid = self.grid
         for k in range(1, grid.side):
             self.push(grid.me, grid.at(k, 0))
             self.push(grid.me, grid.at(0, k))
@@ -81,14 +92,19 @@
     def relay_second(self):
         grid = self.grid
         for j in range(1, grid.side):
-            owner = grid.at(0, j)
-            self.wait(owner)
-            self.push(owner, grid.sibling())
-        for j in range(1, grid.side):
-            for k in range(1, grid.side):
+            for k in range(grid.side):
                 owner = grid.at(k, j)
                 self.wait(owner)
                 self.push(owner, grid.sibling())
+
+    def relay(self):
+        grid = self.grid
+        for j in range(grid.side):
+            for k in range(grid.side):
+                if j or k:
+                    owner = grid.at(k, j)
+                    self.wait(owner)
+                    self.push(owner, grid.sibling())
 
     def take(self):
         grid = self.grid
@@ -142,8 +158,7 @@
     hacc,
     own_terms,
     snd,
-    from_left,
-    from_right,
+    boxes,
     scores,
     probs,
     tops,
@@ -171,6 +186,8 @@
     modes = rates_ref.shape[0]
     steps = rows // SEGS
     wide = wfull.shape[3]
+    part = wfull.shape[2]
+    w_cuts = W_CUTS if part % (16 * W_CUTS) == 0 else 1
     f32 = jnp.float32
     me, z = lax.axis_index("ctx"), lax.axis_index("tp")
     grid = Grid(ctx, me)
@@ -219,36 +236,53 @@
         paired = z + (j // 2 + 1) * (1 if j % 2 else -1)
         return jnp.where(j < 2 * shorter, paired, z + (j - shorter + 1) * longer_way)
 
-    def w_copy(j):
+    def w_rows(r):
+        return pl.ds(r * (part // w_cuts), part // w_cuts)
+
+    def w_copy(j, r):
         other = near(j)
         return remote(
-            w_hbm.at[me, :, pl.ds(pl.multiple_of(other * wide, wide), wide)],
-            wfull.at[z, me],
-            wz_sems.at[0, j],
-            wz_sems.at[1, z],
+            w_hbm.at[me, w_rows(r), pl.ds(pl.multiple_of(other * wide, wide), wide)],
+            wfull.at[z, me, w_rows(r), :],
+            wz_sems.at[0, r, j],
+            wz_sems.at[1, r, z],
             {"tp": other},
         )
 
-    def w_wait(j):
-        source = near(j)
-        remote(
-            w_hbm.at[me, :, pl.ds(0, wide)], wfull.at[source, me], wz_sems.at[0, j], wz_sems.at[1, source], {"tp": source}
-        ).wait_recv()
-
-    def w_gather(j):
+    def w_gather(j, r):
         source = near(j)
         return Gather(
             grid,
-            lambda o: wfull.at[source, o],
-            lambda i: wx_send.at[j, i],
-            lambda o: wx_recv.at[j, o],
+            lambda o: wfull.at[source, o, w_rows(r), :],
+            lambda i: wx_send.at[r, j, i],
+            lambda o: wx_recv.at[r, j, o],
         )
+
+    def w_own(j, lines):
+        for r in range(w_cuts):
+            source = near(j)
+            remote(
+                w_hbm.at[me, w_rows(r), pl.ds(0, wide)],
+                wfull.at[source, me, w_rows(r), :],
+                wz_sems.at[0, r, j],
+                wz_sems.at[1, r, source],
+                {"tp": source},
+            ).wait_recv()
+            if lines:
+                w_parts[j][r].own_lines()
+            else:
+                w_parts[j][r].own()
+
+    def w_each(j, act):
+        for item in w_parts[j]:
+            act(item)
 
     others = range(tp - 1)
     hops = range(1, tp)
-    w_parts = [w_gather(j) for j in others]
+    w_parts = [[w_gather(j, r) for r in range(w_cuts)] for j in others]
     for j in others:
-        w_copy(j).start()
+        for r in range(w_cuts):
+            w_copy(j, r).start()
     for load in loads[7:]:
         load.start()
 
@@ -260,6 +294,9 @@
         )
 
     val_parts = [val_gather(h) for h in range(HALVES)]
+
+    loads[5].wait()
+    key_part.own_lines()
 
     for load in loads[:5]:
         load.wait()
@@ -329,8 +366,7 @@
         lax.fori_loop(0, count, step, 0)
 
     each(ctx - 1 - me, lambda i: end_copy(i + 1).start())
-    w_wait(0)
-    w_parts[0].own()
+    w_own(0, True)
     each(me, end_wait)
 
     def mix_block(i, unused):
@@ -363,23 +399,43 @@
 
     lax.fori_loop(0, blocks, mix_block, 0)
 
-    def gat_copy(source, h, way):
+    def gat_copy(source, c, way, hop):
+        tall = half // GAT_CUTS
+        place = gat.at[source, c // GAT_CUTS, pl.ds(c % GAT_CUTS * tall, tall), :]
         return remote(
-            gat.at[source, h],
-            gat.at[source, h],
-            gat_send.at[h, way, source],
-            gat_recv.at[h, source],
-            {"tp": jnp.clip(z + 1 - 2 * way, 0, tp - 1)},
+            place,
+            place,
+            gat_send.at[c, way, hop, source],
+            gat_recv.at[c, source],
+            {"tp": jnp.clip(z + (hop + 1) * (1 - 2 * way), 0, tp - 1)},
         )
 
-    def gat_give(source, h, way):
-        @pl.when((z < tp - 1) if way == 0 else (z > 0))
+    def place_of(way):
+        return z if way == 0 else tp - 1 - z
+
+    def gat_pass(source, c, way, here, act):
+        p = place_of(way)
+
+        @pl.when(here & (p % 2 == 0) & (p + 2 < tp))
         def _():
-            gat_copy(source, h, way).start()
-
-    def gat_own(h):
+            act(gat_copy(source, c, way, 1))
+
+        @pl.when(here & (((p % 2 == 0) | (source == z)) & (p + 1 < tp)))
+        def _():
+            act(gat_copy(source, c, way, 0))
+
+    def gat_own(c, act=lambda copy: copy.start()):
         for way in range(2):
-            gat_give(z, h, way)
+            gat_pass(z, c, way, z >= 0, act)
+
+    def gat_more(c, j, act=lambda copy: copy.start()):
+        source = near(j)
+        gat_pass(source, c, 0, source < z, act)
+        gat_pass(source, c, 1, source > z, act)
+
+    def gat_step(c, j):
+        gat_copy(near(j), c, 0, 0).wait_recv()
+        gat_more(c, j)
 
     def project(source, h, start):
         term = jnp.dot(
@@ -390,62 +446,64 @@
         else:
             hacc[...] += term
 
-    def gat_step(h, j):
-        source = near(j)
-        gat_copy(source, h, 0).wait_recv()
-
-        @pl.when((source < z) & (z < tp - 1))
-        def _():
-            gat_copy(source, h, 0).start()
-
-        @pl.when((source > z) & (z > 0))
-        def _():
-            gat_copy(source, h, 1).start()
-
     def all_terms(h):
         hyena = hacc[...].astype(jnp.bfloat16)
         hyena_ref[h * half : (h + 1) * half, :] = hyena
         for d in range(tp):
-            own_terms[d] = jnp.dot(
+            own_terms[h, d] = jnp.dot(
                 hyena_ref[h * half : (h + 1) * half, :], vv[d], preferred_element_type=f32
             )
 
-    def sum_copy(d, h, way):
-        box = from_left if way == 0 else from_right
+    def sum_rows(c):
+        tall = half // SUM_CUTS
+        return pl.ds(c % SUM_CUTS * tall, tall)
+
+    def sum_copy(d, c, way, hop):
+        h, at = c // SUM_CUTS, sum_rows(c)
         return remote(
-            snd.at[h, d],
-            box.at[h, d],
-            sum_send.at[h, d],
-            sum_recv.at[h, way, d],
-            {"tp": jnp.clip(z + 1 - 2 * way, 0, tp - 1)},
+            snd.at[h, d, at, :],
+            boxes.at[way, hop - 1, h, d, at, :],
+            sum_send.at[c, d],
+            sum_recv.at[c, way, hop - 1, d],
+            {"tp": jnp.clip(z + hop * (1 - 2 * way), 0, tp - 1)},
         )
 
-    def sum_step(h, k):
+    def sum_add(d, c, way, hop):
+        h, at = c // SUM_CUTS, sum_rows(c)
+
+        @pl.when(place_of(way) >= hop)
+        def _():
+            sum_copy(d, c, way, hop).wait_recv()
+            own_terms[h, d, at, :] += boxes[way, hop - 1, h, d, at, :].astype(f32)
+
+    def sum_hop(k, way):
+        return jnp.where(place_of(way) % 2 == 1, min(k, 2), 1)
+
+    def sum_step(c, k, odd):
+        h, at = c // SUM_CUTS, sum_rows(c)
         for way in range(2):
-            d = z + k if way == 0 else z - k
-
-            @pl.when((d < tp) if way == 0 else (d >= 0))
+            d = z + k * (1 - 2 * way)
+            p = place_of(way)
+
+            @pl.when((p + k < tp) & (p % 2 == odd))
             def _():
-                box = from_left if way == 0 else from_right
-
-                @pl.when((z > 0) if way == 0 else (z < tp - 1))
+                if odd:
+                    sum_add(d, c, way, 1)
+                    if tp > 4:
+                        sum_add(d, c, way, 2)
+                snd[h, d, at, :] = own_terms[h, d, at, :].astype(jnp.bfloat16)
+                sum_copy(d, c, way, sum_hop(k, way)).start()
+
+    def sum_last(h):
+        for c in range(h * SUM_CUTS, (h + 1) * SUM_CUTS):
+            for way in range(2):
+                sum_add(z, c, way, 1)
+
+                @pl.when(place_of(way) % 2 == 1)
                 def _():
-                    sum_copy(d, h, way).wait_recv()
-                    own_terms[d] += box[h, d].astype(f32)
-
-                snd[h, d] = own_terms[d].astype(jnp.bfloat16)
-                sum_copy(d, h, way).start()
-
-    def sum_last(h):
-        for way in range(2):
-            box = from_left if way == 0 else from_right
-
-            @pl.when((z > 0) if way == 0 else (z < tp - 1))
-            def _():
-                sum_copy(z, h, way).wait_recv()
-                own_terms[z] += box[h, z].astype(f32)
-
-        vals[me, h] = own_terms[z].astype(jnp.bfloat16)
+                    sum_add(z, c, way, 2)
+
+        vals[me, h] = own_terms[h, z].astype(jnp.bfloat16)
         val_parts[h].own()
 
     scale = math.log2(math.e) / math.sqrt(HD)
@@ -502,54 +560,59 @@
         acc = lax.fori_loop(0, me + 1, step, jnp.zeros((rows, HD), f32))
         out_ref[:, here] = (acc / totals[head]).astype(jnp.bfloat16)
 
-    loads[5].wait()
     gat_own(0)
-    gat_own(1)
-    w_wait(1)
-    w_parts[1].own()
-    w_parts[0].relay_first()
-    for j in others[2:]:
-        w_wait(j)
-        w_parts[j].own()
-    for j in others[1:]:
-        w_parts[j].relay_first()
-    gat_step(0, 0)
-    key_part.own()
-    for j in others:
-        w_parts[j].relay_second()
-    for load in loads[6:]:
+    key_part.relay_first()
+    w_own(1, True)
+    w_each(0, Gather.relay_first)
+    key_part.relay_second()
+    key_part.take()
+    loads[6].wait()
+    weigh(0)
+    w_each(0, Gather.relay_second)
+    w_each(1, Gather.relay_first)
+    for load in loads[7:]:
         load.wait()
     project(z, 0, True)
-    for j in others[1:]:
+    for j in others[2:]:
+        w_own(j, False)
+    gat_step(0, 0)
+    gat_own(1)
+    weigh(1)
+    w_each(1, Gather.relay_second)
+    w_each(0, Gather.take)
+    project(near(0), 0, False)
+    gat_step(0, 1)
+    w_each(1, Gather.take)
+    project(near(1), 0, False)
+    for j in others[2:]:
+        w_each(j, Gather.relay)
         gat_step(0, j)
-    for j in others:
-        w_parts[j].take()
+        w_each(j, Gather.take)
         project(near(j), 0, False)
     all_terms(0)
+    for k in reversed(hops):
+        sum_step(0, k, 0)
     gat_step(1, 0)
-    sum_step(0, tp - 1)
-    key_part.relay_first()
-    for j in others[1:]:
+    gat_step(1, 1)
+    for head in range(2, heads):
+        weigh(head)
+    for k in reversed(hops):
+        sum_step(0, k, 1)
+    for j in others[2:]:
         gat_step(1, j)
-        sum_step(0, tp - 1 - j)
-    key_part.relay_second()
     project(z, 1, True)
     for j in others:
         project(near(j), 1, False)
-    sum_last(0)
     all_terms(1)
     for k in reversed(hops):
-        sum_step(1, k)
-        if k == tp - 1:
-            val_parts[0].relay_first()
-            key_part.take()
-    val_parts[0].relay_second()
+        sum_step(1, k, 0)
+    sum_last(0)
+    for k in reversed(hops):
+        sum_step(1, k, 1)
+    val_parts[0].relay()
+    sum_last(1)
     val_parts[0].take()
-    for head in range(heads):
-        weigh(head)
-    sum_last(1)
-    val_parts[1].relay_first()
-    val_parts[1].relay_second()
+    val_parts[1].relay()
     val_parts[1].take()
     for head in range(heads):
         blend(head)
@@ -560,35 +623,23 @@
 
     each(ctx - 1 - me, lambda i: end_copy(i + 1).wait_send())
     for j in others:
-        w_copy(j).wait_send()
-        w_parts[j].finish()
+        for r in range(w_cuts):
+            w_copy(j, r).wait_send()
+        w_each(j, Gather.finish)
     key_part.finish()
     for h in range(HALVES):
         val_parts[h].finish()
-        for way in range(2):
-
-            @pl.when((z < tp - 1) if way == 0 else (z > 0))
-            def _():
-                gat_copy(z, h, way).wait_send()
-
+    for c in range(HALVES * GAT_CUTS):
+        gat_own(c, lambda copy: copy.wait_send())
         for j in others:
-            source = near(j)
-
-            @pl.when((source < z) & (z < tp - 1))
-            def _():
-                gat_copy(source, h, 0).wait_send()
-
-            @pl.when((source > z) & (z > 0))
-            def _():
-                gat_copy(source, h, 1).wait_send()
-
+            gat_more(c, j, lambda copy: copy.wait_send())
+    for c in range(HALVES * SUM_CUTS):
         for k in hops:
             for way in range(2):
-                d = z + k if way == 0 else z - k
-
-                @pl.when((d < tp) if way == 0 else (d >= 0))
+
+                @pl.when(place_of(way) + k < tp)
                 def _():
-                    sum_copy(d, h, way).wait_send()
+                    sum_copy(z + k * (1 - 2 * way), c, way, 1).wait_send()
 
 
 def shards(streams, short_filter, decay_rates, residues, skip_gain, hyena_weight, value_weight, queries, key_vectors):
@@ -634,10 +685,9 @@
             vmem((ctx, rows, width), bf16),
             vmem((ctx, HALVES, half, width), bf16),
             vmem((half, wide), f32),
-            vmem((tp, half, width), f32),
+            vmem((HALVES, tp, half, width), f32),
             vmem((HALVES, tp, half, width), bf16),
-            vmem((HALVES, tp, half, width), bf16),
-            vmem((HALVES, tp, half, width), bf16),
+            vmem((2, 2, HALVES, tp, half, width), bf16),
             vmem((ctx, rows, rows), f32),
             vmem((heads, ctx, rows, rows), bf16),
             vmem((rows, HD), f32),
@@ -645,17 +695,17 @@
             dma((8 + tp,)),
             dma((2,)),
             dma((2, ctx)),
-            dma((2, tp)),
-            dma((tp, ctx)),
-            dma((tp, ctx)),
+            dma((2, W_CUTS, tp)),
+            dma((W_CUTS, tp, ctx)),
+            dma((W_CUTS, tp, ctx)),
             dma((ctx,)),
             dma((ctx,)),
             dma((HALVES, ctx)),
             dma((HALVES, ctx)),
-            dma((HALVES, 2, tp)),
-            dma((HALVES, tp)),
-            dma((HALVES, tp)),
-            dma((HALVES, 2, tp)),
+            dma((HALVES * GAT_CUTS, 2, 2, tp)),
+            dma((HALVES * GAT_CUTS, tp)),
+            dma((HALVES * SUM_CUTS, tp)),
+            dma((HALVES * SUM_CUTS, 2, 2, tp)),
         ],
         cost_estimate=pl.CostEstimate(
             flops=4 * rows * ctx * rows * width,

time: 89 us -> 85 us (0.955)
  the two profiles are of different devices: /device:TPU:0 before, /device:TPU:15 now
where the time goes in v2:
time: 85 us; the launch traced here: 84.8 us
  Pallas kernels  80.6 us (95%)
  local copies, waits for them, and re-layouts  3.54 us (4%)
    pallas_call x1, Pallas kernels, shards(): pl.pallas_call(functools.partial(body, ctx, tp), in_specs=[pl.BlockSpec(m...  80.6 us
    unnamed x2, local copies, waits for them, and re-layouts  3.54 us

profile of v2, /device:TPU:15, one launch (start us, length us, event | category | flops | bytes accessed | tf_op | source)
XLA Modules:
  0.0 84.8 jit_solution(14012835347269342266)
XLA Ops:
  0.6 80.6 %hyena_attention.1 = (bf16[256,1024]{1,0:T(8,128)(2,1)}, bf16[256,512]{1,0:T(8,128)(2,1)}) custom-call(bf16[3,256,512]{2,1,0:T(8,128)(2,1)} %streams_hbm.1, f32[3,7,512]{2,1,0:T(8,128)} %taps_hbm.1, f32[16,512]{1,0:T(8,128)} %bitcast.5, f32[16,512]{1,0:T(8,128)} %bitcast.6, f32[1,512]{1,0:T(1,128)} %bitcast.7, bf16[8,64,4096]{2,1,0:T(8,128)(2,1)} %bitcast.4, ...), custom_call_target="tpu_custom_call" | custom-call | flops 1073741824 | bytes 4194304 | tf_op jit(solution)/shard_map/hyena_attention/pallas_call | solution.py:660
  81.2 1.9 %copy.13 = bf16[256,1024]{1,0:T(8,128)(2,1)} copy(bf16[256,1024]{1,0:T(8,128)(2,1)} %get-tuple-element.4) | data formatting | bytes 1048576
  83.1 1.7 %copy.14 = bf16[256,512]{1,0:T(8,128)(2,1)} copy(bf16[256,512]{1,0:T(8,128)(2,1)} %get-tuple-element.5) | data formatting | bytes 524288

commit v3 on v2

--- a/solution.py
+++ b/solution.py
@@ -150,6 +150,7 @@
     first,
     ends,
     gat,
+    w_own_rows,
     wfull,
     vv,
     q_ref,
@@ -207,7 +208,11 @@
         pltpu.make_async_copy(v_hbm.at[:, pl.ds(d * width, width)], vv.at[d], loc_sems.at[8 + d])
         for d in range(tp)
     ]
-    for load in loads[:7]:
+    shares = [
+        pltpu.make_async_copy(w_hbm.at[me, :, pl.ds(d * wide, wide)], w_own_rows.at[d], loc_sems.at[8 + tp + d])
+        for d in range(tp)
+    ]
+    for load in shares + loads[:7]:
         load.start()
 
     barrier = pltpu.get_barrier_semaphore()
@@ -233,7 +238,7 @@
     longer_way = jnp.where(z < tp - 1 - z, 1, -1)
 
     def near(j):
-        paired = z + (j // 2 + 1) * (1 if j % 2 else -1)
+        paired = z + (j // 2 + 1) * (2 * (j % 2) - 1)
         return jnp.where(j < 2 * shorter, paired, z + (j - shorter + 1) * longer_way)
 
     def w_rows(r):
@@ -242,7 +247,7 @@
     def w_copy(j, r):
         other = near(j)
         return remote(
-            w_hbm.at[me, w_rows(r), pl.ds(pl.multiple_of(other * wide, wide), wide)],
+            w_own_rows.at[other, w_rows(r), :],
             wfull.at[z, me, w_rows(r), :],
             wz_sems.at[0, r, j],
             wz_sems.at[1, r, z],
@@ -262,7 +267,7 @@
         for r in range(w_cuts):
             source = near(j)
             remote(
-                w_hbm.at[me, w_rows(r), pl.ds(0, wide)],
+                w_own_rows.at[source, w_rows(r), :],
                 wfull.at[source, me, w_rows(r), :],
                 wz_sems.at[0, r, j],
                 wz_sems.at[1, r, source],
@@ -279,10 +284,13 @@
 
     others = range(tp - 1)
     hops = range(1, tp)
+    for load in shares:
+        load.wait()
     w_parts = [[w_gather(j, r) for r in range(w_cuts)] for j in others]
     for j in others:
+        turn = jnp.where((shorter == 0) & (j > 0), tp - 1 - j, j)
         for r in range(w_cuts):
-            w_copy(j, r).start()
+            w_copy(turn, r).start()
     for load in loads[7:]:
         load.start()
 
@@ -594,8 +602,7 @@
         sum_step(0, k, 0)
     gat_step(1, 0)
     gat_step(1, 1)
-    for head in range(2, heads):
-        weigh(head)
+    weigh(2) if heads > 2 else None
     for k in reversed(hops):
         sum_step(0, k, 1)
     for j in others[2:]:
@@ -607,6 +614,8 @@
     for k in reversed(hops):
         sum_step(1, k, 0)
     sum_last(0)
+    for head in range(3, heads):
+        weigh(head)
     for k in reversed(hops):
         sum_step(1, k, 1)
     val_parts[0].relay()
@@ -679,6 +688,7 @@
             vmem((modes * SEGS, LANES), f32),
             vmem((ctx, blocks, modes, LANES), f32),
             vmem((tp, HALVES, half, chans), bf16),
+            vmem((tp, part, wide), bf16),
             vmem((tp, ctx, part, wide), bf16),
             vmem((tp, deep, width), bf16),
             vmem((rows, width), bf16),
@@ -692,7 +702,7 @@
             vmem((heads, ctx, rows, rows), bf16),
             vmem((rows, HD), f32),
             vmem((heads, rows, HD), f32),
-            dma((8 + tp,)),
+            dma((8 + 2 * tp,)),
             dma((2,)),
             dma((2, ctx)),
             dma((2, W_CUTS, tp)),

time: 85 us -> 84.8 us (level)
  no operation moved by 1% of the time
where the time goes in v3:
time: 84.8 us; the launch traced here: 84.6 us
  Pallas kernels  80.4 us (95%)
  local copies, waits for them, and re-layouts  3.54 us (4%)
    pallas_call x1, Pallas kernels, shards(): pl.pallas_call(functools.partial(body, ctx, tp), in_specs=[pl.BlockSpec(m...  80.4 us
    unnamed x2, local copies, waits for them, and re-layouts  3.54 us

profile of v3, /device:TPU:15, one launch (start us, length us, event | category | flops | bytes accessed | tf_op | source)
XLA Modules:
  0.0 84.6 jit_solution(279960224438317729)
XLA Ops:
  0.6 80.4 %hyena_attention.1 = (bf16[256,1024]{1,0:T(8,128)(2,1)}, bf16[256,512]{1,0:T(8,128)(2,1)}) custom-call(bf16[3,256,512]{2,1,0:T(8,128)(2,1)} %streams_hbm.1, f32[3,7,512]{2,1,0:T(8,128)} %taps_hbm.1, f32[16,512]{1,0:T(8,128)} %bitcast.5, f32[16,512]{1,0:T(8,128)} %bitcast.6, f32[1,512]{1,0:T(1,128)} %bitcast.7, bf16[8,64,4096]{2,1,0:T(8,128)(2,1)} %bitcast.4, ...), custom_call_target="tpu_custom_call" | custom-call | flops 1073741824 | bytes 4194304 | tf_op jit(solution)/shard_map/hyena_attention/pallas_call | solution.py:669
  81.0 1.9 %copy.13 = bf16[256,1024]{1,0:T(8,128)(2,1)} copy(bf16[256,1024]{1,0:T(8,128)(2,1)} %get-tuple-element.4) | data formatting | bytes 1048576
  82.9 1.7 %copy.14 = bf16[256,512]{1,0:T(8,128)(2,1)} copy(bf16[256,512]{1,0:T(8,128)(2,1)} %get-tuple-element.5) | data formatting | bytes 524288

commit v4 on v3

--- a/solution.py
+++ b/solution.py
@@ -557,16 +557,21 @@
         each(me + 1, weight)
         totals[head] = jnp.broadcast_to(jnp.sum(totals[head], axis=1, keepdims=True), tops.shape)
 
-    def blend(head):
-        here = slice(head * HD, (head + 1) * HD)
-
-        def step(b, acc):
-            return acc + jnp.dot(
-                probs[head, b], vals[b, :, :, here].reshape(rows, HD), preferred_element_type=f32
+    def blend():
+        def step(b, sums):
+            return tuple(
+                sums[head]
+                + jnp.dot(
+                    probs[head, b],
+                    vals[b, :, :, head * HD : (head + 1) * HD].reshape(rows, HD),
+                    preferred_element_type=f32,
+                )
+                for head in range(heads)
             )
 
-        acc = lax.fori_loop(0, me + 1, step, jnp.zeros((rows, HD), f32))
-        out_ref[:, here] = (acc / totals[head]).astype(jnp.bfloat16)
+        sums = lax.fori_loop(0, me + 1, step, (jnp.zeros((rows, HD), f32),) * heads)
+        for head in range(heads):
+            out_ref[:, head * HD : (head + 1) * HD] = (sums[head] / totals[head]).astype(jnp.bfloat16)
 
     gat_own(0)
     key_part.relay_first()
@@ -623,8 +628,7 @@
     val_parts[0].take()
     val_parts[1].relay()
     val_parts[1].take()
-    for head in range(heads):
-        blend(head)
+    blend()
 
     @pl.when(me < ctx - 1)
     def _():

time: 84.8 us -> 82.5 us (0.973)
  Pallas kernels: 80.4 us -> 77.4 us
    pallas_call x1, Pallas kernels: 80.4 us -> 77.4 us  [shards(): pl.pallas_call(functools.partial(body, ctx, tp), in_specs=[pl.BlockSpec(m...]
where the time goes in v4:
time: 82.5 us; the launch traced here: 81.6 us
  Pallas kernels  77.4 us (94%)
  local copies, waits for them, and re-layouts  3.54 us (4%)
    pallas_call x1, Pallas kernels, shards(): pl.pallas_call(functools.partial(body, ctx, tp), in_specs=[pl.BlockSpec(m...  77.4 us
    unnamed x2, local copies, waits for them, and re-layouts  3.54 us

profile of v4, /device:TPU:15, one launch (start us, length us, event | category | flops | bytes accessed | tf_op | source)
XLA Modules:
  0.0 81.6 jit_solution(3995101304269246254)
XLA Ops:
  0.6 77.4 %hyena_attention.1 = (bf16[256,1024]{1,0:T(8,128)(2,1)}, bf16[256,512]{1,0:T(8,128)(2,1)}) custom-call(bf16[3,256,512]{2,1,0:T(8,128)(2,1)} %streams_hbm.1, f32[3,7,512]{2,1,0:T(8,128)} %taps_hbm.1, f32[16,512]{1,0:T(8,128)} %bitcast.5, f32[16,512]{1,0:T(8,128)} %bitcast.6, f32[1,512]{1,0:T(1,128)} %bitcast.7, bf16[8,64,4096]{2,1,0:T(8,128)(2,1)} %bitcast.4, ...), custom_call_target="tpu_custom_call" | custom-call | flops 1073741824 | bytes 4194304 | tf_op jit(solution)/shard_map/hyena_attention/pallas_call | solution.py:673
  78.1 1.9 %copy.13 = bf16[256,1024]{1,0:T(8,128)(2,1)} copy(bf16[256,1024]{1,0:T(8,128)(2,1)} %get-tuple-element.4) | data formatting | bytes 1048576
  79.9 1.7 %copy.14 = bf16[256,512]{1,0:T(8,128)(2,1)} copy(bf16[256,512]{1,0:T(8,128)(2,1)} %get-tuple-element.5) | data formatting | bytes 524288
